TPU v7x, 32 devices: a whole 2x2x4 slice. The times are simulated.
32 devices in a mesh: sub: 8 (over z, x), lvl: 4 (over y, core).
Axes of the slice: x: 2, y: 2, z: 4, core: 2. Of those that a mesh axis runs over, the one named last changes fastest.
Arguments:
- vectors: bfloat16 [1024, 2, 256], P(('sub', 'lvl')), may hold values from -6 to 6
- self_blocks: bfloat16 [1024, 256, 256], P(('sub', 'lvl')), may hold values from -0.375 to 0.375
- near_blocks: bfloat16 [1024, 256, 256], P(('sub', 'lvl')), may hold values from -0.375 to 0.375
- near_row: int32 [1024], P(('sub', 'lvl')), may hold values from 0 to 31
- near_col: int32 [1024], P(('sub', 'lvl')), may hold values from 0 to 63
- bases: bfloat16 [1024, 256, 64], P(('sub', 'lvl')), may hold values from -0.375 to 0.375
- transfers: float32 [1984, 64, 64], P(('sub', 'lvl')), may hold values from -0.5 to 0.5
- far_row: int32 [4096], P(('sub', 'lvl')), may hold values from 0 to 31
- far_col: int32 [4096], P(('sub', 'lvl')), may hold values from 0 to 1023, as said below
- couplings: float32 [4096, 64, 64], P(('sub', 'lvl')), may hold values from -0.75 to 0.75
- root_couplings: float32 [32, 32, 64, 64], P(('sub', 'lvl')), may hold values from -1.5 to 1.5
Outputs:
- products: float32 [1024, 2, 256], P(('sub', 'lvl'))
Inputs may be any that keep to these rules, and one draw needn't show every extreme that they name: `far_col`: the column leaf of an admissible pair never lies on the owning device. Of each device's 128 pairs, exactly 16 have column leaves on each of the six devices 1, 2 or 3 places before or after it (cyclically over all devices). The others lie on devices more than 3 places away, at most 16 on any one device, and exactly 16 of them on one such device.
All inputs are finite; a program needn't handle non-finite values.
Results may differ from a plain program's by a relative error of at most 0.0024.
Values may be sent and summed in bfloat16 or wider, within the bound.
No kernel may reach another device: no remote copies, remote signals or barrier semaphores. Data moves between devices by JAX's collectives and lax.ppermute only.
A program may use at most 128 MiB of HBM per device.

v0:
```python
import jax
import jax.numpy as jnp
from jax import lax
from jax.sharding import PartitionSpec as P

HIGH = lax.Precision.HIGHEST


def from_behind(x, axis, by):
    devices = lax.axis_size(axis)
    return lax.ppermute(x, axis, [(i, (i + by) % devices) for i in range(devices)])


def tree_levels(count):
    levels = []
    offset = 0
    width = count
    while width > 1:
        levels.append((offset, width))
        offset += width
        width //= 2
    return levels


def tree_up(coeff, trans):
    for offset, width in tree_levels(coeff.shape[0]):
        prod = jnp.einsum("nvk,nkr->nvr", coeff, trans[offset : offset + width], precision=HIGH)
        coeff = prod.reshape(width // 2, 2, 2, prod.shape[-1]).sum(axis=1)
    return coeff[0]


def tree_down(top, leaf_terms, trans):
    field = top[None]
    for offset, width in reversed(tree_levels(leaf_terms.shape[0])):
        field = jnp.einsum(
            "nkr,nvr->nvk",
            trans[offset : offset + width],
            jnp.repeat(field, 2, axis=0),
            precision=HIGH,
        )
    return field + leaf_terms


def one_hot(index, count):
    slots = lax.broadcasted_iota(jnp.int32, (count, index.shape[0]), 0)
    return (slots == index[None, :]).astype(jnp.float32)


def shards(
    vectors,
    self_blocks,
    near_blocks,
    near_row,
    near_col,
    bases,
    transfers,
    far_row,
    far_col,
    couplings,
    root_couplings,
):
    count = vectors.shape[0]
    rank = bases.shape[2]
    pairs = far_row.shape[0]
    devices = lax.axis_size(("sub", "lvl"))
    coeff = jnp.einsum("lvi,lik->lvk", vectors, bases, preferred_element_type=jnp.float32)
    flat = coeff.reshape(count, 2 * rank)
    root = tree_up(coeff, transfers)
    roots = lax.all_gather(root.reshape(1, 2 * rank), ("sub", "lvl"), axis=0, tiled=True)
    root_field = jnp.einsum(
        "erk,evk->vr", root_couplings[0], roots.reshape(devices, 2, rank), precision=HIGH
    )
    following = from_behind(vectors, ("sub", "lvl"), -1)
    both = jnp.concatenate([vectors, following], axis=0)
    forward = jnp.einsum(
        "pij,pvj->pvi", near_blocks, both[near_col], preferred_element_type=jnp.float32
    )
    backward = jnp.einsum(
        "pij,pvi->pvj", near_blocks, vectors[near_row], preferred_element_type=jnp.float32
    )
    self_out = jnp.einsum("lij,lvj->lvi", self_blocks, vectors, preferred_element_type=jnp.float32)
    near_own = jnp.einsum("lp,pvi->lvi", one_hot(near_row, count), forward, precision=HIGH)
    back_all = jnp.einsum("lp,pvj->lvj", one_hot(near_col, 2 * count), backward, precision=HIGH)
    returned = from_behind(back_all[count:], ("sub", "lvl"), 1)
    near_part = self_out + near_own + back_all[:count] + returned
    gathered = lax.all_gather(flat, ("sub", "lvl"), axis=0, tiled=True)
    partner = gathered[far_col]
    far_forward = jnp.einsum(
        "prk,pvk->pvr", couplings, partner.reshape(pairs, 2, rank), precision=HIGH
    )
    leaf_field = jnp.einsum("lp,pvr->lvr", one_hot(far_row, count), far_forward, precision=HIGH)
    far_backward = jnp.einsum("prk,pvr->pvk", couplings, coeff[far_row], precision=HIGH).reshape(
        pairs, 2 * rank
    )
    incoming = lax.psum_scatter(
        jnp.dot(
            one_hot(far_col, lax.axis_size(("sub", "lvl")) * count), far_backward, precision=HIGH
        ),
        ("sub", "lvl"),
        scatter_dimension=0,
        tiled=True,
    )
    leaf_field = leaf_field + incoming.reshape(count, 2, rank)
    field = tree_down(root_field, leaf_field, transfers).astype(jnp.bfloat16)
    far_part = jnp.einsum("lik,lvk->lvi", bases, field, preferred_element_type=jnp.float32)
    return near_part + far_part


def solution(mesh):
    in_specs = (
        P(("sub", "lvl"), None, None),
        P(("sub", "lvl"), None, None),
        P(("sub", "lvl"), None, None),
        P(("sub", "lvl")),
        P(("sub", "lvl")),
        P(("sub", "lvl"), None, None),
        P(("sub", "lvl"), None, None),
        P(("sub", "lvl")),
        P(("sub", "lvl")),
        P(("sub", "lvl"), None, None),
        P(("sub", "lvl"), None, None, None),
    )
    out_specs = P(("sub", "lvl"), None, None)
    return jax.shard_map(shards, mesh=mesh, in_specs=in_specs, out_specs=out_specs, check_vma=False)
```

profile of v0, /device:TPU:0, one launch (start us, length us, event | category | flops | bytes accessed | tf_op | source)
XLA Modules:
  0.0 172.8 jit_solution(13755800622901884387)
XLA Ops:
  6.5 6.4 %collective-permute-start = (bf16[32,2,256]{2,1,0:T(2,128)(2,1)}, bf16[32,2,256]{2,1,0:T(2,128)(2,1)S(1)}, u32[]{:S(2)}, u32[]{:S(2)}) collective-permute-start(bf16[32,2,256]{2,1,0:T(2,128)(2,1)} %param.11), channel_id=1, source_target_pairs={{0,31},{1,0},{2,1},{3,2},{4,3},{5,4},{6,5},{7,6},{8,7},{9,8},{10,9... | collective-permute-start | bytes 98312 | tf_op jit(solution)/shard_map/ppermute | solution.py:11
  12.9 1.2 fusion.44
  14.1 5.6 %copy.29 = f32[128,64,64]{2,1,0:T(8,128)} copy(f32[128,64,64]{0,2,1:T(8,128)} %param.20) | data formatting | bytes 4194304 | tf_op args[9]
  19.7 0.7 gather_fusion.3
  20.5 5.3 %fusion.46 = f32[128,2,64]{2,1,0:T(2,128)S(1)} fusion(f32[128,2,64]{2,1,0:T(2,128)S(1)} %gather_fusion.3, f32[128,64,64]{2,1,0:T(8,128)} %copy.29), kind=kOutput, calls=%fused_computation.69 | convolution fusion | flops 12582912 | bytes 2228224 | tf_op jit(solution)/shard_map/prk,pvr->pvk/dot_general | solution.py:92
  25.9 1.2 fusion.8
  27.1 0.6 gather_fusion.1
  27.8 2.8 %fusion.43 = f32[32,2,256]{2,1,0:T(2,128)S(1)} fusion(bf16[32,2,256]{2,1,0:T(2,128)(2,1)S(1)} %gather_fusion.1, bf16[32,256,256]{2,1,0:T(8,128)(2,1)} %param.13), kind=kOutput, calls=%fused_computation.66 | convolution fusion | flops 8388608 | bytes 4292608 | tf_op jit(solution)/shard_map/pij,pvi->pvj/dot_general | solution.py:78
  31.2 39.6 %all_gather.7 = f32[1024,128]{1,0:T(8,128)S(1)} all-gather(f32[32,128]{1,0:T(8,128)S(1)} %reshape.59), channel_id=1, replica_groups=mesh['sub'=8,'lvl'=4] {'sub','lvl'}, dimensions={0}, use_global_device_ids=true | all-gather | bytes 540672 | tf_op jit(solution)/shard_map/all_gather | solution.py:86
  70.8 0.6 gather_fusion.2
  71.6 8.5 %fusion.45 = f32[128,2,64]{2,1,0:T(2,128)S(1)} fusion(f32[128,2,64]{2,1,0:T(2,128)S(1)} %copy.28, f32[128,64,64]{2,1,0:T(8,128)} %copy.29), kind=kOutput, calls=%fused_computation.68 | convolution fusion | flops 12582912 | bytes 2228224 | tf_op jit(solution)/shard_map/prk,pvk->pvr/dot_general | solution.py:88
  80.3 1.0 bitcast_reduce_fusion
  81.3 0.5 bitcast_reduce_fusion.1
  82.7 36.7 %all-gather = f32[32,1,128]{2,1,0:T(1,128)S(1)} all-gather(f32[1,1,128]{2,1,0:T(1,128)S(1)} %reshape.99), channel_id=1, replica_groups=mesh['sub'=8,'lvl'=4] {'sub','lvl'}, dimensions={0}, use_global_device_ids=true | all-gather | bytes 16896 | tf_op jit(solution)/shard_map/all_gather | solution.py:69
  119.9 0.7 reduce.5
  120.7 2.1 %convolution_bitcast_fusion = f32[2,64]{1,0:T(2,128)S(1)} fusion(f32[32,2,64]{2,1,0:T(2,128)S(1)} %reshape.53, f32[1,32,64,64]{3,2,1,0:T(8,128)} %param.21), kind=kOutput, calls=%fused_computation.10 | convolution fusion | flops 3145728 | bytes 541184 | tf_op jit(solution)/shard_map/erk,evk->vr/dot_general | solution.py:70
  123.4 0.5 fusion.14
  124.0 0.9 fusion.9
  125.0 0.6 gather_fusion
  125.6 3.4 %fusion.42 = f32[32,2,256]{2,1,0:T(2,128)S(1)} fusion(bf16[32,2,256]{2,1,0:T(2,128)(2,1)S(1)} %gather_fusion, bf16[32,256,256]{2,1,0:T(8,128)(2,1)} %param.13), kind=kOutput, calls=%fused_computation.65 | convolution fusion | flops 8388608 | bytes 4292608 | tf_op jit(solution)/shard_map/pij,pvj->pvi/dot_general | solution.py:75
  129.2 29.9 %reduce-scatter.2.cloned.1.call-done = f32[32,128]{1,0:T(8,128)} async-done(((f32[1024,128]{1,0:T(8,128)}), f32[32,128]{1,0:T(8,128)}) %reduce-scatter.2.cloned.1.call-update) | async-done | bytes 16400 | tf_op jit(solution)/shard_map/reduce_scatter | solution.py:95
  159.1 0.8 reshape.62
  159.9 1.7 %fusion.3 = bf16[32,2,64]{2,1,0:T(2,128)(2,1)S(1)} fusion(f32[32,2,64]{2,1,0:T(2,128)S(1)} %bitcast.57, f32[62,64,64]{2,1,0:T(8,128)S(1)} %copy-done.1, f32[32,2,64]{2,1,0:T(2,128)S(1)} %reshape.62, f32[32,2,64]{2,0,1:T(8,128)S(1)} %fusion.18), kind=kOutput, calls=%fused_computation.9 | convolution fusion | flops 3158016 | bytes 1155072 | tf_op jit(solution)/shard_map/nkr,nvr->nvk/dot_general | solution.py:35
  161.9 4.0 %fusion.2 = f32[32,2,256]{2,1,0:T(2,128)} fusion(f32[32,2,256]{2,1,0:T(2,128)S(1)} %fusion.47, f32[32,2,256]{2,1,0:T(2,128)S(1)} %collective-permute-done.1, bf16[32,2,256]{2,1,0:T(2,128)(2,1)S(1)} %copy-done.2, bf16[32,256,256]{2,1,0:T(8,128)(2,1)} %param.12, f32[32,2,256]{2,0,1:T(8,128)S(1)} %get-tuple-element.5, f32[32,2,256]{2,0,1:T(8,128)S(1)} %fusion.26), kind=kOutput, calls=%fused_computation.7 | convolution fusion | flops 8454144 | bytes 4554752 | tf_op jit(solution)/shard_map/lij,lvj->lvi/dot_general | solution.py:81
  (50 shorter events, 3.7 us)
Async XLA Ops:
  6.5 6.4 %copy-start = (bf16[32,256,64]{1,2,0:T(8,128)(2,1)S(1)}, bf16[32,256,64]{1,2,0:T(8,128)(2,1)}, u32[]{:S(2)}) copy-start(bf16[32,256,64]{1,2,0:T(8,128)(2,1)} %param.16) | copy-start | bytes 3145732
  6.5 152.5 %reduce-scatter.2.cloned.1.call-start = ((), (), s32[]{:S(2)}) async-start(), calls=%async_computation.1 | async-start | bytes 540672 | tf_op jit(solution)/shard_map/reduce_scatter | solution.py:95
  6.5 118.4 %collective-permute-start = (bf16[32,2,256]{2,1,0:T(2,128)(2,1)}, bf16[32,2,256]{2,1,0:T(2,128)(2,1)S(1)}, u32[]{:S(2)}, u32[]{:S(2)}) collective-permute-start(bf16[32,2,256]{2,1,0:T(2,128)(2,1)} %param.11), channel_id=1, source_target_pairs={{0,31},{1,0},{2,1},{3,2},{4,3},{5,4},{6,5},{7,6},{8,7},{9,8},{10,9... | collective-permute-start | bytes 98312 | tf_op jit(solution)/shard_map/ppermute | solution.py:11
  14.1 5.6 %copy-start.3 = (s32[128]{0:T(128)S(1)}, s32[128]{0:T(128)}, u32[]{:S(2)}) copy-start(s32[128]{0:T(128)} %param.18) | copy-start | bytes 1540
  20.4 5.4 %copy-start.6 = (s32[128]{0:T(128)S(1)}, s32[128]{0:T(128)}, u32[]{:S(2)}) copy-start(s32[128]{0:T(128)} %param.19) | copy-start | bytes 1540
  20.4 6.6 %copy-start.5 = (s32[32]{0:T(128)S(1)}, s32[32]{0:T(128)}, u32[]{:S(2)}) copy-start(s32[32]{0:T(128)} %param.14) | copy-start | bytes 388
  20.5 6.6 %copy-start.2 = (bf16[32,2,256]{2,1,0:T(2,128)(2,1)S(1)}, bf16[32,2,256]{2,1,0:T(2,128)(2,1)}, u32[]{:S(2)}) copy-start(bf16[32,2,256]{2,1,0:T(2,128)(2,1)} %param.11) | copy-start | bytes 98308
  27.7 2.9 %copy-start.4 = (s32[32]{0:T(128)S(1)}, s32[32]{0:T(128)}, u32[]{:S(2)}) copy-start(s32[32]{0:T(128)} %param.15) | copy-start | bytes 388
  31.0 130.9 %collective-permute-start.1 = (f32[32,2,256]{2,1,0:T(2,128)S(1)}, f32[32,2,256]{2,1,0:T(2,128)S(1)}, u32[]{:S(2)}, u32[]{:S(2)}) collective-permute-start(f32[32,2,256]{2,1,0:T(2,128)S(1)} %copy.35), channel_id=1, source_target_pairs={{0,1},{1,2},{2,3},{3,4},{4,5},{5,6},{6,7},{7,8},{8,9},{9,10},{10,1... | collective-permute-start | bytes 196616 | tf_op jit(solution)/shard_map/ppermute | solution.py:11
  71.6 8.7 %copy-start.1 = (f32[62,64,64]{2,1,0:T(8,128)S(1)}, f32[62,64,64]{2,1,0:T(8,128)}, u32[]{:S(2)}) copy-start(f32[62,64,64]{2,1,0:T(8,128)} %param.17) | copy-start | bytes 3047428
Sparse Core Ops, SparseCore 0:
  27.2 131.8 reduce-scatter.1
where the time goes:
time: 173 us
  blocking collectives  76.3 us (44%)
  matrix products  35.5 us (21%)
  waiting for transfers between devices  29.9 us (17%)
  between operations  13.6 us (8%)
  local copies, waits for them, and re-layouts  10.3 us (6%)
  starting transfers between devices  6.43 us (4%)
    all_gather x1, blocking collectives, shards(): gathered = lax.all_gather(flat, ('sub', 'lvl'), axis=0, tiled=True)  39.6 us
    all_gather x1, blocking collectives, shards(): lax.all_gather(root.reshape(1, 2 * rank), ('sub', 'lvl'), axis=0, tiled=T...  36.7 us
    reduce_scatter x1, waiting for transfers between devices, shards(): lax.psum_scatter(jnp.dot(one_hot(far_col, lax.axis_size(('sub', 'lvl')) *...  29.9 us
    dot_general x1, matrix products, shards(): jnp.einsum('prk,pvk->pvr', couplings, partner.reshape(pairs, 2, rank), pr...  8.46 us
    ppermute x2, starting transfers between devices, from_behind(): lax.ppermute(x, axis, [(i, (i + by) % devices) for i in range(devices)])  6.43 us
    unnamed x17, local copies, waits for them, and re-layouts  5.78 us
    dot_general x1, matrix products, shards(): jnp.einsum('prk,pvr->pvk', couplings, coeff[far_row], precision=HIGH)  5.29 us
    dot_general x1, matrix products, shards(): jnp.einsum('lij,lvj->lvi', self_blocks, vectors, preferred_element_type=j...  4.02 us
  transfers between devices with their start and end apart: 3, of which 1 were waited for; matrix products, arithmetic and copies ran while one was open for 25% of the time, Pallas kernels for 0%

commit v1 on v0

v1 whole, which is shorter than its diff:
```python
import jax
import jax.numpy as jnp
from jax import lax
from jax.experimental import pallas as pl
from jax.experimental.pallas import tpu as pltpu
from jax.sharding import PartitionSpec as P

AXES = ("sub", "lvl")
F32 = jnp.float32
BF16 = jnp.bfloat16
NN = (((1,), (0,)), ((), ()))
NT = (((1,), (1,)), ((), ()))


def from_behind(x, by):
    devices = lax.axis_size(AXES)
    return lax.ppermute(x, AXES, [(i, (i + by) % devices) for i in range(devices)])


def iota(shape, dim):
    return lax.broadcasted_iota(jnp.int32, shape, dim)


def mul(a, b, dims):
    return lax.dot_general(a, b, dims, preferred_element_type=F32)


def split(x):
    high = x.astype(BF16)
    return high, (x - high.astype(F32)).astype(BF16)


def mul_split(a, b, dims):
    a_high, a_low = split(a)
    b_high, b_low = split(b)
    rows = a.shape[0]
    both = mul(jnp.concatenate([a_high, a_low], axis=0), b_high, dims)
    return both[:rows] + both[rows:] + mul(a_high, b_low, dims)


def mul_exact_left(a, b, dims):
    b_high, b_low = split(b)
    return mul(a, b_high, dims) + mul(a, b_low, dims)


def turn(x):
    rows = x.shape[0]
    if rows < 128:
        x = jnp.concatenate([x, jnp.zeros((128 - rows, x.shape[1]), x.dtype)], axis=0)
    return x.T


def swap_halves(x):
    return pltpu.roll(x, x.shape[-1] // 2, x.ndim - 1)


def chosen(condition):
    return jnp.where(condition, 1.0, 0.0).astype(BF16)


def reverse_bits(x, bits):
    out = jnp.zeros_like(x)
    for b in range(bits):
        out = out | (((x >> b) & 1) << (bits - 1 - b))
    return out


def own_leaf(rows, wide, count):
    leaf = lax.rem(iota((rows, wide), 0), count)
    half = iota((rows, wide), 1) // (wide // 2)
    return leaf, half


def start_all(pairs, sems):
    copies = [pltpu.make_async_copy(src, dst, sems.at[i]) for i, (src, dst) in enumerate(pairs)]
    for copy in copies:
        copy.start()
    return copies


def pack_kernel(
    row_in, col_in, x_in, bases_in, trans_in, coup_in, out, far_row, far_col, x, bases, trans, coup, sems
):
    devices, _, wide = out.shape
    count = x.shape[0]
    rows = 2 * count
    rank = wide // 2
    pairs = far_row.shape[1]
    cap = count // 2
    per_row = wide // cap
    copies = start_all(
        [
            (col_in, far_col),
            (row_in, far_row),
            (x_in, x),
            (bases_in, bases),
            (coup_in, coup),
            (trans_in, trans),
        ],
        sems,
    )

    me = lax.axis_index(AXES)
    copies[0].wait()
    dev = far_col[...] // count
    leaf = lax.rem(far_col[...], count)
    dev_along = jnp.broadcast_to(dev.astype(F32), (pairs, pairs))
    earlier = iota((pairs, pairs), 0) < iota((pairs, pairs), 1)
    same = (dev_along == dev_along.T) & earlier
    place = jnp.sum(same.astype(F32), axis=0, keepdims=True).astype(jnp.int32)
    seat = dev * cap + place
    at_seat = jnp.where(iota((devices * cap, pairs), 0) == seat, 1.0, 0.0).astype(BF16)
    of_dev = jnp.where(iota((devices, pairs), 0) == dev, leaf.astype(F32), 0.0).astype(BF16)
    lane_of = place + lax.rem(me, per_row) * cap
    at_lane = jnp.where(iota((wide, pairs), 0) == lane_of, 1.0, 0.0).astype(BF16)
    ids = mul(of_dev, at_lane, NT)
    copies[1].wait()
    bits = count.bit_length() - 1
    of_row = chosen(iota((wide, pairs), 0) == reverse_bits(far_row[...], bits))
    line = iota((rows, rows), 0)
    lane = iota((rows, rows), 1)
    order = reverse_bits(lax.rem(line, count), bits)
    turn_rows = chosen((line // count == lane // count) & (order == lax.rem(lane, count)))

    copies[2].wait()
    turned_x = jnp.concatenate([x[:, 0, :], x[:, 1, :]], axis=0)
    turned_x = mul(turn_rows, turned_x, NN).astype(BF16)
    copies[3].wait()
    prod = mul(turned_x, bases[...], NT)
    row_leaf, half = own_leaf(rows, wide, count)
    row_leaf = reverse_bits(row_leaf, bits)
    coeff = jnp.zeros((rows, wide), F32)
    for c in range(count // 2):
        piece = jnp.where(row_leaf == 2 * c + half, prod[:, c * wide : (c + 1) * wide], 0.0)
        coeff = coeff + piece
    coeff = coeff + swap_halves(coeff)
    half_one = iota((count, wide), 1) < rank
    flat = jnp.where(half_one, coeff[:count], coeff[count:])
    flat_b = flat.astype(BF16)
    for e in range(devices):
        first = e % 2 * cap
        out[e, :cap, :] = flat_b[first : first + cap]

    turned = jnp.concatenate([flat, jnp.zeros((wide - count, wide), F32)], axis=0).T
    t_high, t_low = split(turned)
    picked = mul(t_high, of_row, NN) + mul(t_low, of_row, NN)
    copies[4].wait()
    copies[5].wait()
    acc0 = jnp.zeros((rank, pairs), F32)
    acc1 = jnp.zeros((rank, pairs), F32)
    offset = 0
    width = count
    done = 0
    nodes = [coeff[:count], coeff[count:]]
    while width > 1:
        parents = width // 2
        span = max(8, parents)
        low = iota((span, wide), 1) < rank
        if parents >= 8:
            pairs_of = [jnp.where(low, n[:parents], n[parents:]) for n in nodes]
        else:
            pairs_of = [jnp.where(low, n, pltpu.roll(n, span - parents, 0)) for n in nodes]
        high, rest = split(jnp.concatenate(pairs_of, axis=0))
        left = jnp.concatenate([high.astype(F32), rest.astype(F32)], axis=0)
        row = lax.rem(iota(left.shape, 0), span)
        node = jnp.where(row < parents, reverse_bits(row, parents.bit_length() - 1), -1)
        left = jnp.concatenate(
            [jnp.where(node == c, left, 0.0).astype(BF16) for c in range(parents)], axis=1
        )
        mats_high, mats_low = split(trans[offset : offset + width].reshape(width * rank, rank))
        up = mul(left, mats_high, NN)
        up = up[: 2 * span] + up[2 * span :] + mul(left[: 2 * span], mats_low, NN)
        until = rank if width == 2 else done + rank // 5
        for r in range(done, until):
            block = coup[r]
            acc0 = acc0 + block * picked[r : r + 1]
            acc1 = acc1 + block * picked[rank + r : rank + r + 1]
        done = until
        up = jnp.concatenate([up, up], axis=1)
        nodes = [up[:span], up[span:]]
        offset += width
        width = parents
    terms = jnp.concatenate([acc0, acc1], axis=0).astype(BF16)
    seated = mul(at_seat, terms, NT).astype(BF16)
    for e in range(devices):
        out[e, cap : 2 * cap, :] = seated[e * cap : (e + 1) * cap]
    root = jnp.where(iota((1, wide), 1) < rank, nodes[0][0:1], nodes[1][0:1])
    root_high, root_low = split(root)
    sub = iota((8, wide), 0)
    tail = jnp.where(
        sub == 0,
        root_high.astype(F32),
        jnp.where(sub == 1, root_low.astype(F32), 0.0),
    )
    for e in range(devices):
        out[e, 2 * cap :, :] = jnp.where(sub == 2, ids[e : e + 1], tail).astype(BF16)


def column(ids):
    wide = ids.shape[1]
    if wide < 128:
        ids = jnp.concatenate([ids, jnp.zeros((1, 128 - wide), jnp.int32)], axis=1)
    return jnp.broadcast_to(ids.astype(F32), (128, 128)).T


def by_seat(col, pairs):
    parts = []
    for g in range(pairs // 8):
        parts += [col[8 * g : 8 * g + 8]] * 2
    return jnp.concatenate(parts, axis=0)


def along_seats(seat_col):
    rows = seat_col.shape[0]
    if rows < 128:
        seat_col = jnp.concatenate([seat_col, jnp.zeros((128 - rows, 128), F32)], axis=0)
    return seat_col.T.astype(jnp.int32)


def products(left, blocks, group, dims):
    member = lax.rem(iota((16, blocks.shape[2]), 0), 8)
    acc = jnp.zeros((16, blocks.shape[2]), F32)
    some = left[16 * group : 16 * group + 16]
    for j in range(8):
        acc = jnp.where(member == j, mul(some, blocks[8 * group + j], dims), acc)
    return acc


def seat_grid(shape, dim):
    seat = iota(shape, dim)
    return lax.rem(seat // 8, 2), (seat // 16) * 8 + lax.rem(seat, 8)


def near_back_kernel(
    row_in, col_in, x_in, blocks_in, own, back, near_row, near_col, x, blocks, sems
):
    pairs = blocks.shape[0]
    count = x.shape[0]
    rows = 2 * count
    seats = 2 * pairs
    parts = pairs // 8
    spans = [pl.ds(8 * g, 8) for g in range(parts)]
    copies = start_all(
        [(row_in, near_row), (col_in, near_col), (x_in, x)]
        + [(blocks_in.at[span], blocks.at[span]) for span in spans],
        sems,
    )
    for i in range(3):
        copies[i].wait()
    here = jnp.concatenate([x[:, 0, :], x[:, 1, :]], axis=0)
    row_seat = by_seat(column(near_row[...]), pairs).astype(jnp.int32)
    col_along = along_seats(by_seat(column(near_col[...]), pairs))
    lane = iota((seats, rows), 1)
    seat_v, _ = seat_grid((seats, rows), 0)
    same = (seat_v == lane // count) & (row_seat[:, :rows] == lax.rem(lane, count))
    of_row = mul(chosen(same), here, NN).astype(BF16)
    backward = []
    for g in range(parts):
        copies[3 + g].wait()
        backward.append(products(of_row, blocks, g, NN))
    backward = jnp.concatenate(backward, axis=0)

    line = iota((rows, seats), 0)
    seat_v, _ = seat_grid((rows, seats), 1)
    same_v = seat_v == line // count
    leaf = lax.rem(line, count)
    col_seat = col_along[:rows, :seats]
    to_next = chosen(same_v & (col_seat == leaf + count))
    back[...] = mul_exact_left(to_next, backward, NN).astype(BF16)
    own[...] = mul_exact_left(chosen(same_v & (col_seat == leaf)), backward, NN)


def near_main_kernel(
    row_in, col_in, x_in, after_in, own_in, blocks_in, selfs_in, own, near_row, near_col, x, after, blocks, selfs, sems
):
    pairs = blocks.shape[0]
    count = x.shape[0]
    rows = 2 * count
    seats = 2 * pairs
    parts = pairs // 8
    spans = [pl.ds(8 * g, 8) for g in range(parts)]
    copies = start_all(
        [(row_in, near_row), (col_in, near_col), (x_in, x), (after_in, after)]
        + [(selfs_in.at[span], selfs.at[span]) for span in spans]
        + [(blocks_in.at[span], blocks.at[span]) for span in spans],
        sems,
    )
    for i in range(4):
        copies[i].wait()
    both = jnp.concatenate([part[:, v, :] for part in (x, after) for v in range(2)], axis=0)
    row_along = along_seats(by_seat(column(near_row[...]), pairs))
    col_seat = by_seat(column(near_col[...]), pairs).astype(jnp.int32)
    lane = iota((seats, 2 * rows), 1)
    seat_v, seat_pair = seat_grid((seats, 2 * rows), 0)
    same_v = seat_v == lax.rem(lane // count, 2)
    leaf = (lane // rows) * count + lax.rem(lane, count)
    of_col = mul(chosen(same_v & (col_seat == leaf)), both, NN).astype(BF16)
    of_self = mul(chosen(same_v & (seat_pair == leaf)), both, NN).astype(BF16)
    forward, selfward = [], []
    for g in range(parts):
        copies[4 + g].wait()
        selfward.append(products(of_self, selfs, g, NT))
    for g in range(parts):
        copies[4 + parts + g].wait()
        forward.append(products(of_col, blocks, g, NT))

    line = iota((rows, seats), 0)
    seat_v, seat_pair = seat_grid((rows, seats), 1)
    same_v = seat_v == line // count
    leaf = lax.rem(line, count)
    spots = jnp.concatenate(
        [
            jnp.where(same_v & (row_along[:rows, :seats] == leaf), 1.0, 0.0),
            jnp.where(same_v & (seat_pair == leaf), 1.0, 0.0),
        ],
        axis=1,
    ).astype(BF16)
    own[...] = own_in[...] + mul_exact_left(spots, jnp.concatenate(forward + selfward, axis=0), NN)


def chains_kernel(trans, chains):
    count = trans.shape[0] // 2 + 1
    rank = trans.shape[1]
    low = iota((rank, 2 * rank), 1) < rank
    width = 2
    offset = trans.shape[0] - 2
    paths = [jnp.concatenate([trans[offset + n]] * 2, axis=1) for n in range(2)]
    while width < count:
        width *= 2
        offset -= width
        lower = []
        for path, first in zip(paths, range(offset, offset + width, 2)):
            left = jnp.concatenate(
                split(trans[first : first + 2].reshape(2 * rank, rank)), axis=1
            )
            high, rest = split(path)
            high = high.astype(F32)
            right = jnp.concatenate(
                [jnp.where(low, high, rest.astype(F32)), jnp.where(low, high, 0.0)], axis=0
            ).astype(BF16)
            prod = mul(left, right, NN)
            prod = prod + swap_halves(prod)
            lower += [prod[:rank], prod[rank:]]
        paths = lower
    for c in range(count // 2):
        both = []
        for path in paths[2 * c : 2 * c + 2]:
            high, rest = split(path)
            both.append(jnp.where(low, high.astype(F32), rest.astype(F32)))
        chains[:, c * 2 * rank : (c + 1) * 2 * rank] = jnp.concatenate(both, axis=0).T.astype(BF16)


def partner_rows(far_col, ref, side, count):
    pairs = far_col.shape[1]
    devices, _, wide = ref.shape
    cap = count // 2
    per = wide // cap
    col = column(far_col[...]).astype(jnp.int32)
    leaf = reverse_bits(lax.rem(col, count), count.bit_length() - 1)
    spot = jnp.where(leaf // cap == side, col // count * cap + lax.rem(leaf, cap), -1)
    rows = jnp.zeros((pairs, wide), F32)
    for g in range(devices // per):
        block = ref[g * per : (g + 1) * per, :cap, :].reshape(wide, wide)
        rows = rows + mul(chosen(iota((pairs, wide), 1) + g * wide == spot), block, NN)
    return rows


def collect_kernel(
    col_in, got_in, chains_in, root_in, own, returned, _, partner, arrived, down, near, far_col, got, chains, roots, sems
):
    devices, _, wide = got.shape
    count = arrived.shape[0]
    rank = wide // 2
    cap = count // 2
    per_row = wide // cap
    copies = start_all(
        [(got_in, got), (col_in, far_col), (root_in, roots), (chains_in, chains)], sems
    )
    near[...] = own[...] + returned[...].astype(F32)
    copies[0].wait()
    copies[1].wait()

    tail = got[:, 2 * cap :, :].astype(F32)
    sums = jnp.zeros((count, wide), F32)
    for g in range(devices // per_row):
        ids = jnp.sum(tail[g * per_row : (g + 1) * per_row, 2], axis=0, keepdims=True)
        at = chosen(iota((count, wide), 0) == ids.astype(jnp.int32))
        block = got[g * per_row : (g + 1) * per_row, cap : 2 * cap, :].reshape(wide, wide)
        sums = sums + mul(at, block, NN)
    arrived[...] = sums

    partner[...] = partner_rows(far_col, got, lax.rem(lax.axis_index(AXES), 2), count)

    root_rows = tail[:, 0] + tail[:, 1]
    second = swap_halves(root_rows)
    copies[2].wait()
    acc0 = jnp.zeros((rank, rank), F32)
    acc1 = jnp.zeros((rank, rank), F32)
    for e in range(devices):
        block = roots[e]
        acc0 = acc0 + block * root_rows[e : e + 1, :rank]
        acc1 = acc1 + block * second[e : e + 1, :rank]

    sums = jnp.concatenate([acc0, acc1], axis=1)
    of_v = chosen(iota((16, wide), 0) // 8 == iota((16, wide), 1) // rank)
    top = mul_exact_left(of_v, sums, NT)
    top = jnp.concatenate(split(top), axis=0)
    copies[3].wait()
    both = mul(jnp.concatenate([top, top], axis=1), chains[...], NN)
    down[...] = both[:16] + both[16:]


def finish_kernel(
    far_row,
    far_col,
    sibling_in,
    partner_in,
    arrived,
    down,
    near,
    bases,
    coup,
    out,
    sibling,
    ahead,
    sems,
):
    _, _, wide = sibling.shape
    rows = near.shape[0]
    count = rows // 2
    rank = wide // 2
    pairs = far_row.shape[1]
    start_all([(sibling_in.at[:, pl.ds(0, sibling.shape[1])], sibling)], sems)[0].wait()
    side = 1 - lax.rem(lax.axis_index(AXES), 2)
    partner = (partner_in[...] + partner_rows(far_col, sibling, side, count)).T

    for r in range(rank):
        block = coup[r]
        ahead[r : r + 1, :] = jnp.sum(block * partner[:rank], axis=0, keepdims=True)
        ahead[rank + r : rank + r + 1, :] = jnp.sum(block * partner[rank:], axis=0, keepdims=True)
    of_row = chosen(iota((count, pairs), 0) == far_row[...])
    leaf_field = arrived[...] + mul_exact_left(of_row, ahead[...], NT)

    leaf_rows = jnp.concatenate([leaf_field, swap_halves(leaf_field)], axis=0)
    leaf_both = jnp.where(iota((rows, wide), 1) < rank, leaf_rows, swap_halves(leaf_rows))
    row_leaf, half = own_leaf(rows, wide, count)
    first = iota((rows, wide), 0) < count
    left = []
    for c in range(count // 2):
        part = down[:, c * wide : (c + 1) * wide]
        part = jnp.where(first, part[0:1], part[8:9]) + leaf_both
        left.append(jnp.where(row_leaf == 2 * c + half, part, 0.0).astype(BF16))
    total = near[...] + mul(jnp.concatenate(left, axis=1), bases[...], NN)
    for v in range(2):
        out[:, v, :] = total[v * count : (v + 1) * count]


def vmem(x):
    return pltpu.VMEM(x.shape, x.dtype)


IN_VMEM = pl.BlockSpec(memory_space=pltpu.VMEM)
IN_HBM = pl.BlockSpec(memory_space=pltpu.HBM)
ANYWHERE = pl.BlockSpec(memory_space=pl.ANY)
ALL = pltpu.CompilerParams(vmem_limit_bytes=60 * 1024 * 1024)
MOST = pltpu.CompilerParams(vmem_limit_bytes=53 * 1024 * 1024)
SOME = pltpu.CompilerParams(vmem_limit_bytes=40 * 1024 * 1024)


def cost(flops, moved):
    return pl.CostEstimate(flops=flops, bytes_accessed=moved, transcendentals=0)


def pack(devices, far_row, far_col, vectors, bases, trans, coup):
    count = vectors.shape[0]
    wide = 2 * trans.shape[2]
    operands = (far_row, far_col, vectors, bases, trans, coup)
    return pl.pallas_call(
        pack_kernel,
        out_shape=jax.ShapeDtypeStruct((devices, count + 8, wide), BF16),
        in_specs=[IN_HBM] * 6,
        out_specs=IN_VMEM,
        scratch_shapes=[vmem(a) for a in operands] + [pltpu.SemaphoreType.DMA((6,))],
        compiler_params=ALL,
        cost_estimate=cost(10**7, 6 * 10**6),
        name="pack",
    )(*operands)


def near_back(near_row, near_col, x, blocks):
    count, _, leaf = x.shape
    operands = (near_row, near_col, x, blocks)
    return pl.pallas_call(
        near_back_kernel,
        out_shape=(
            jax.ShapeDtypeStruct((2 * count, leaf), F32),
            jax.ShapeDtypeStruct((2 * count, leaf), BF16),
        ),
        in_specs=[IN_HBM] * 4,
        out_specs=(IN_VMEM, IN_VMEM),
        scratch_shapes=[vmem(a) for a in operands]
        + [pltpu.SemaphoreType.DMA((3 + blocks.shape[0] // 8,))],
        compiler_params=MOST,
        cost_estimate=cost(10**7, 4 * 10**6),
        name="near_back",
    )(*operands)


def near_main(near_row, near_col, x, after, own, blocks, selfs):
    fetched = (near_row, near_col, x, after, blocks, selfs)
    return pl.pallas_call(
        near_main_kernel,
        out_shape=jax.ShapeDtypeStruct(own.shape, F32),
        in_specs=[IN_HBM] * 4 + [IN_VMEM] + [IN_HBM] * 2,
        out_specs=IN_VMEM,
        scratch_shapes=[vmem(a) for a in fetched]
        + [pltpu.SemaphoreType.DMA((4 + 2 * (blocks.shape[0] // 8),))],
        compiler_params=MOST,
        cost_estimate=cost(2 * 10**7, 8 * 10**6),
        name="near_main",
    )(near_row, near_col, x, after, own, blocks, selfs)


def multiply_chains(trans):
    nodes, rank, _ = trans.shape
    leaves = nodes // 2 + 1
    return pl.pallas_call(
        chains_kernel,
        out_shape=jax.ShapeDtypeStruct((2 * rank, leaves * rank), BF16),
        in_specs=[IN_VMEM],
        out_specs=IN_VMEM,
        compiler_params=SOME,
        cost_estimate=cost(10**7, 3 * 10**6),
        name="chains",
    )(trans)


def collect(far_col, got, chains, roots, own, returned, sign, count):
    wide = got.shape[2]
    fetched = (far_col, got, chains, roots)
    return pl.pallas_call(
        collect_kernel,
        out_shape=(
            jax.ShapeDtypeStruct((far_col.shape[1], wide), F32),
            jax.ShapeDtypeStruct((count, wide), F32),
            jax.ShapeDtypeStruct((16, chains.shape[1]), F32),
            jax.ShapeDtypeStruct(own.shape, F32),
        ),
        in_specs=[IN_HBM] * 4 + [IN_VMEM] * 2 + [ANYWHERE],
        out_specs=(IN_VMEM,) * 4,
        scratch_shapes=[vmem(a) for a in fetched] + [pltpu.SemaphoreType.DMA((4,))],
        compiler_params=MOST,
        cost_estimate=cost(10**7, 3 * 10**6),
        name="collect",
    )(far_col, got, chains, roots, own, returned, sign)


def finish(far_row, far_col, sibling, partner, arrived, down, near, bases, coup):
    count = near.shape[0] // 2
    devices, _, wide = sibling.shape
    halves = jax.ShapeDtypeStruct((devices, count // 2, wide), BF16)
    return pl.pallas_call(
        finish_kernel,
        out_shape=jax.ShapeDtypeStruct((count, 2, near.shape[1]), F32),
        in_specs=[IN_VMEM] * 2 + [IN_HBM] + [IN_VMEM] * 6,
        out_specs=IN_VMEM,
        scratch_shapes=[
            vmem(halves),
            pltpu.VMEM((wide, far_row.shape[1]), F32),
            pltpu.SemaphoreType.DMA((1,)),
        ],
        compiler_params=SOME,
        cost_estimate=cost(10**7, 5 * 10**6),
        name="finish",
    )(far_row, far_col, sibling, partner, arrived, down, near, bases, coup)


def shards(
    vectors,
    self_blocks,
    near_blocks,
    near_row,
    near_col,
    bases,
    transfers,
    far_row,
    far_col,
    couplings,
    root_couplings,
):
    count, _, leaf = vectors.shape
    rank = bases.shape[2]
    pairs = far_row.shape[0]
    devices = lax.axis_size(AXES)

    flat_bases = bases.transpose(0, 2, 1).reshape(count * rank, leaf)
    coup = couplings.transpose(1, 2, 0)
    far = (far_row.reshape(1, pairs), far_col.reshape(1, pairs))
    near = (near_row.reshape(1, -1), near_col.reshape(1, -1))
    following = from_behind(vectors, -1)
    payload = pack(devices, *far, vectors, flat_bases, transfers, coup)
    payload, following, x = lax.optimization_barrier((payload, following, vectors))
    got = lax.all_to_all(payload, AXES, 0, 0, tiled=True)
    own, back = near_back(*near, x, near_blocks)
    returned = from_behind(back, 1)
    own = near_main(*near, x, following, own, near_blocks, self_blocks)
    own, late_transfers = lax.optimization_barrier((own, transfers))
    chains = multiply_chains(late_transfers)
    got, chains, sign = lax.optimization_barrier((got, chains, returned[:8]))
    sibling = lax.ppermute(got, AXES, [(i, i ^ 1) for i in range(devices)])
    partner, arrived, down, near_sum = collect(
        far[1], got, chains, root_couplings[0], own, returned, sign, count
    )
    return finish(*far, sibling, partner, arrived, down, near_sum, flat_bases, coup)


def solution(mesh):
    in_specs = (
        P(AXES, None, None),
        P(AXES, None, None),
        P(AXES, None, None),
        P(AXES),
        P(AXES),
        P(AXES, None, None),
        P(AXES, None, None),
        P(AXES),
        P(AXES),
        P(AXES, None, None),
        P(AXES, None, None, None),
    )
    out_specs = P(AXES, None, None)
    return jax.shard_map(shards, mesh=mesh, in_specs=in_specs, out_specs=out_specs, check_vma=False)
```

time: 173 us -> 31.8 us (0.18)
  blocking collectives: 76.3 us -> 0 us
  matrix products: 35.5 us -> 0 us
  waiting for transfers between devices: 29.9 us -> 1.93 us
  Pallas kernels: 0 us -> 17.8 us
  between operations: 13.6 us -> 0.16 us
  local copies, waits for them, and re-layouts: 10.3 us -> 2.19 us
  starting transfers between devices: 6.43 us -> 9.46 us
    all_gather x2 -> x0, blocking collectives: 76.3 us -> none  [the longest x1 39.6 us: shards(): gathered = lax.all_gather(flat, ('sub', 'lvl'), axis=0, tiled=True)]
    dot_general x22 -> x0, matrix products: 35.5 us -> none  [the longest x1 8.46 us: shards(): jnp.einsum('prk,pvk->pvr', couplings, partner.reshape(pairs, 2, rank), pr...]
    reduce_scatter x1 -> x0, waiting for transfers between devices: 29.9 us -> none  [shards(): lax.psum_scatter(jnp.dot(one_hot(far_col, lax.axis_size(('sub', 'lvl')) *...]
    pallas_call x0 -> x6, Pallas kernels: none -> 17.8 us  [the longest x1 4.81 us: near_main(): pl.pallas_call(near_main_kernel, out_shape=jax.ShapeDtypeStruct(own.shape...]
    unnamed x17 -> x22, local copies, waits for them, and re-layouts: 5.78 us -> 2.18 us
    gather x5 -> x0, local copies, waits for them, and re-layouts: 2.74 us -> none  [the longest x1 0.74 us: shards(): coeff[far_row]]
    all_to_all x0 -> x1, starting transfers between devices: none -> 2.73 us  [shards(): got = lax.all_to_all(payload, AXES, 0, 0, tiled=True)]
    ppermute x2 -> x3, waiting for transfers between devices: 0.02 us -> 1.92 us  [the longest x2 1.92 us: from_behind(): lax.ppermute(x, AXES, [(i, (i + by) % devices) for i in range(devices)])]
  transfers between devices with their start and end apart: 3 -> 4, of which waited for: 1 -> 1; matrix products, arithmetic and copies ran while one was open for 25% -> 0% of each run, Pallas kernels for 0% -> 50%
where the time goes in v1:
time: 31.8 us; the launch traced here: 31.5 us
  Pallas kernels  17.8 us (56%)
  starting transfers between devices  9.46 us (30%)
  local copies, waits for them, and re-layouts  2.19 us (7%)
  waiting for transfers between devices  1.93 us (6%)
    ppermute x2, starting transfers between devices, from_behind(): lax.ppermute(x, AXES, [(i, (i + by) % devices) for i in range(devices)])  6.73 us
    pallas_call x1, Pallas kernels, near_main(): pl.pallas_call(near_main_kernel, out_shape=jax.ShapeDtypeStruct(own.shape...  4.81 us
    pallas_call x1, Pallas kernels, pack(): pl.pallas_call(pack_kernel, out_shape=jax.ShapeDtypeStruct((devices, coun...  4.77 us
    all_to_all x1, starting transfers between devices, shards(): got = lax.all_to_all(payload, AXES, 0, 0, tiled=True)  2.73 us
    pallas_call x1, Pallas kernels, near_back(): pl.pallas_call(near_back_kernel, out_shape=(jax.ShapeDtypeStruct((2 * cou...  2.7 us
    unnamed x22, local copies, waits for them, and re-layouts  2.18 us
    pallas_call x1, Pallas kernels, finish(): pl.pallas_call(finish_kernel, out_shape=jax.ShapeDtypeStruct((count, 2, n...  2.02 us
    pallas_call x1, Pallas kernels, collect(): pl.pallas_call(collect_kernel, out_shape=(jax.ShapeDtypeStruct((far_col.s...  2.02 us
  transfers between devices with their start and end apart: 4, of which 1 were waited for; matrix products, arithmetic and copies ran while one was open for 0% of the time, Pallas kernels for 50%

profile of v1, /device:TPU:0, one launch (start us, length us, event | category | flops | bytes accessed | tf_op | source)
XLA Modules:
  0.0 31.5 jit_solution(3325525893874020372)
XLA Ops:
  0.0 6.4 %collective-permute-start = (bf16[32,2,256]{2,1,0:T(2,128)(2,1)}, bf16[32,2,256]{2,1,0:T(2,128)(2,1)S(1)}, u32[]{:S(2)}, u32[]{:S(2)}) collective-permute-start(bf16[32,2,256]{2,1,0:T(2,128)(2,1)} %x_in.3), channel_id=1, source_target_pairs={{0,31},{1,0},{2,1},{3,2},{4,3},{5,4},{6,5},{7,6},{8,7},{9,8},{10,9... | collective-permute-start | bytes 98312 | tf_op jit(solution)/shard_map/ppermute | solution.py:17
  6.4 4.8 %pack.1 = bf16[32,40,128]{2,1,0:T(8,128)(2,1)} custom-call(s32[1,128]{1,0:T(1,128)} %bitcast.20, s32[1,128]{1,0:T(1,128)} %bitcast.13, bf16[32,2,256]{2,1,0:T(2,128)(2,1)} %x_in.3, bf16[2048,256]{1,0:T(8,128)(2,1)} %bitcast.11, f32[62,64,64]{2,1,0:T(8,128)} %trans, f32[64,64,128]{2,1,0:T(8,128)} %bitcast.9), custom_call_target="tpu_custom_call" | custom-call | flops 10000000 | bytes 6000000 | tf_op jit(solution)/shard_map/pack/pallas_call | solution.py:478
  11.2 0.0 collective-permute-done.after_in
  11.2 2.7 %all-to-all-start = ((bf16[32,40,128]{2,1,0:T(8,128)(2,1)}), bf16[32,40,128]{2,1,0:T(8,128)(2,1)S(1)}, u32[]{:S(2)}, u32[]{:S(2)}) async-start(bf16[32,40,128]{2,1,0:T(8,128)(2,1)} %pack.1), calls=%async_computation | async-start | bytes 655360 | tf_op jit(solution)/shard_map/all_to_all | solution.py:603
  14.0 0.0 copy-done.4
  14.0 0.0 copy-done.9
  14.0 2.7 %near_back.1 = (f32[64,256]{1,0:T(8,128)S(1)}, bf16[64,256]{1,0:T(8,128)(2,1)S(1)}) custom-call(s32[1,32]{1,0:T(1,128)S(1)} %bitcast.16, s32[1,32]{1,0:T(1,128)S(1)} %bitcast.18, bf16[32,2,256]{2,1,0:T(2,128)(2,1)S(1)} %copy-done.4, bf16[32,256,256]{2,1,0:T(8,128)(2,1)} %blocks_in.3), custom_call_target="tpu_custom_call" | custom-call | flops 10000000 | bytes 4000000 | tf_op jit(solution)/shard_map/near_back/pallas_call | solution.py:493
  16.7 0.3 collective-permute-start.1
  17.0 4.8 %near_main.1.own = f32[64,256]{1,0:T(8,128)S(1)} custom-call(s32[1,32]{1,0:T(1,128)S(1)} %bitcast.17, s32[1,32]{1,0:T(1,128)S(1)} %bitcast.19, bf16[32,2,256]{2,1,0:T(2,128)(2,1)S(1)} %copy-done.4, bf16[32,2,256]{2,1,0:T(2,128)(2,1)S(1)} %collective-permute-done.after_in, f32[64,256]{1,0:T(8,128)S(1)} %get-tuple-element.22.own_in, ...), custom_call_target="tpu_custom_call" | custom-call | flops 20000000 | bytes 8000000 | tf_op jit(solution)/shard_map/near_main/pallas_call | solution.py:511
  21.8 0.0 copy-start
  21.8 0.0 copy-start.2
  21.9 1.4 %chains.1.chains_in = bf16[128,2048]{1,0:T(8,128)(2,1)S(1)} custom-call(f32[62,64,64]{2,1,0:T(8,128)S(1)} %copy-done.1), custom_call_target="tpu_custom_call" | custom-call | flops 10000000 | bytes 3000000 | tf_op jit(solution)/shard_map/chains/pallas_call | solution.py:527
  23.3 0.0 copy-start.3
  23.3 0.8 %copy-done.3 = bf16[128,2048]{1,0:T(8,128)(2,1)} copy-done((bf16[128,2048]{1,0:T(8,128)(2,1)}, bf16[128,2048]{1,0:T(8,128)(2,1)S(1)}, u32[]{:S(2)}) %copy-start.3) | copy-done | bytes 524312
  24.1 1.9 %collective-permute-done.1.returned = bf16[64,256]{1,0:T(8,128)(2,1)S(1)} collective-permute-done((bf16[64,256]{1,0:T(8,128)(2,1)S(1)}, bf16[64,256]{1,0:T(8,128)(2,1)S(1)}, u32[]{:S(2)}, u32[]{:S(2)}) %collective-permute-start.1) | collective-permute-done | bytes 32800 | tf_op jit(solution)/shard_map/ppermute | solution.py:17
  26.0 0.6 %copy-done.5 = bf16[64,256]{1,0:T(8,128)(2,1)} copy-done((bf16[64,256]{1,0:T(8,128)(2,1)}, bf16[64,256]{1,0:T(8,128)(2,1)S(1)}, u32[]{:S(2)}) %copy-start.5) | copy-done | bytes 32792
  26.6 0.0 all-to-all-done.got_in
  26.6 0.0 collective-permute-start.2
  26.6 0.0 copy-done.7
  26.6 0.0 copy-start.6
  26.7 0.7 %copy-done.6 = bf16[64,256]{1,0:T(8,128)(2,1)S(1)} copy-done((bf16[64,256]{1,0:T(8,128)(2,1)S(1)}, bf16[64,256]{1,0:T(8,128)(2,1)}, u32[]{:S(2)}) %copy-start.6) | copy-done | bytes 32792
  27.4 2.0 %collect.1 = (f32[128,128]{1,0:T(8,128)S(1)}, f32[32,128]{1,0:T(8,128)S(1)}, f32[16,2048]{1,0:T(8,128)S(1)}, f32[64,256]{1,0:T(8,128)S(1)}) custom-call(s32[1,128]{1,0:T(1,128)S(1)} %bitcast.14, bf16[32,40,128]{2,1,0:T(8,128)(2,1)S(1)} %all-to-all-done.got_in, bf16[128,2048]{1,0:T(8,128)(2,1)} %copy-done.3, f32[32,64,64]{2,1,0:T(8,128)} %bitcast.22, ...), custom_call_target="tpu_custom_call" | custom-call | flops 10000000 | bytes 3000000 | tf_op jit(solution)/shard_map/collect/pallas_call | solution.py:541
  29.4 0.0 collective-permute-done.2.sibling_in
  29.5 2.0 %finish.1 = f32[32,2,256]{2,1,0:T(2,128)} custom-call(s32[1,128]{1,0:T(1,128)S(1)} %bitcast.21, s32[1,128]{1,0:T(1,128)S(1)} %bitcast.15, bf16[32,40,128]{2,1,0:T(8,128)(2,1)S(1)} %collective-permute-done.2.sibling_in, f32[128,128]{1,0:T(8,128)S(1)} %get-tuple-element.29.partner_in, f32[32,128]{1,0:T(8,128)S(1)} %get-tuple-element.30.arrived, ...), custom_call_target="tpu_custom_call" | custom-call | flops 10000000 | bytes 5000000 | tf_op jit(solution)/shard_map/finish/pallas_call | solution.py:562
  (13 shorter events, 0.0 us)
Async XLA Ops:
  0.0 14.0 %copy-start.4 = (bf16[32,2,256]{2,1,0:T(2,128)(2,1)S(1)}, bf16[32,2,256]{2,1,0:T(2,128)(2,1)}, u32[]{:S(2)}) copy-start(bf16[32,2,256]{2,1,0:T(2,128)(2,1)} %x_in.3) | copy-start | bytes 98308
  0.0 14.0 %copy-start.9 = (s32[32]{0:T(128)S(1)}, s32[32]{0:T(128)}, u32[]{:S(2)}) copy-start(s32[32]{0:T(128)} %param.15) | copy-start | bytes 388
  0.0 14.0 %copy-start.8 = (s32[32]{0:T(128)S(1)}, s32[32]{0:T(128)}, u32[]{:S(2)}) copy-start(s32[32]{0:T(128)} %param.14) | copy-start | bytes 388
  0.0 11.2 %collective-permute-start = (bf16[32,2,256]{2,1,0:T(2,128)(2,1)}, bf16[32,2,256]{2,1,0:T(2,128)(2,1)S(1)}, u32[]{:S(2)}, u32[]{:S(2)}) collective-permute-start(bf16[32,2,256]{2,1,0:T(2,128)(2,1)} %x_in.3), channel_id=1, source_target_pairs={{0,31},{1,0},{2,1},{3,2},{4,3},{5,4},{6,5},{7,6},{8,7},{9,8},{10,9... | collective-permute-start | bytes 98312 | tf_op jit(solution)/shard_map/ppermute | solution.py:17
  11.2 15.4 %all-to-all-start = ((bf16[32,40,128]{2,1,0:T(8,128)(2,1)}), bf16[32,40,128]{2,1,0:T(8,128)(2,1)S(1)}, u32[]{:S(2)}, u32[]{:S(2)}) async-start(bf16[32,40,128]{2,1,0:T(8,128)(2,1)} %pack.1), calls=%async_computation | async-start | bytes 655360 | tf_op jit(solution)/shard_map/all_to_all | solution.py:603
  16.7 9.3 %collective-permute-start.1 = (bf16[64,256]{1,0:T(8,128)(2,1)S(1)}, bf16[64,256]{1,0:T(8,128)(2,1)S(1)}, u32[]{:S(2)}, u32[]{:S(2)}) collective-permute-start(bf16[64,256]{1,0:T(8,128)(2,1)S(1)} %get-tuple-element.24), channel_id=1, source_target_pairs={{0,1},{1,2},{2,3},{3,4},{4,5},{5,6},{6,7},{7,8},{8,9},{9,10},{10,1... | collective-permute-start | bytes 98312 | tf_op jit(solution)/shard_map/ppermute | solution.py:17
  17.0 4.8 %copy-start.1 = (f32[62,64,64]{2,1,0:T(8,128)S(1)}, f32[62,64,64]{2,1,0:T(8,128)}, u32[]{:S(2)}) copy-start(f32[62,64,64]{2,1,0:T(8,128)} %trans) | copy-start | bytes 3047428
  17.0 9.6 %copy-start.7 = (s32[128]{0:T(128)S(1)}, s32[128]{0:T(128)}, u32[]{:S(2)}) copy-start(s32[128]{0:T(128)} %param.19) | copy-start | bytes 1540
  17.0 12.4 %copy-start.10 = (s32[128]{0:T(128)S(1)}, s32[128]{0:T(128)}, u32[]{:S(2)}) copy-start(s32[128]{0:T(128)} %param.18) | copy-start | bytes 1540
  21.8 7.6 %copy-start = (f32[128,64,64]{0,2,1:T(8,128)S(1)}, f32[128,64,64]{0,2,1:T(8,128)}, u32[]{:S(2)}) copy-start(f32[128,64,64]{0,2,1:T(8,128)} %param.20) | copy-start | bytes 6291460
  21.8 7.6 %copy-start.2 = (bf16[32,256,64]{1,2,0:T(8,128)(2,1)S(1)}, bf16[32,256,64]{1,2,0:T(8,128)(2,1)}, u32[]{:S(2)}) copy-start(bf16[32,256,64]{1,2,0:T(8,128)(2,1)} %param.16) | copy-start | bytes 3145732
  23.3 0.8 %copy-start.3 = (bf16[128,2048]{1,0:T(8,128)(2,1)}, bf16[128,2048]{1,0:T(8,128)(2,1)S(1)}, u32[]{:S(2)}) copy-start(bf16[128,2048]{1,0:T(8,128)(2,1)S(1)} %chains.1.chains_in) | copy-start | bytes 1572868
  26.0 0.6 %copy-start.5 = (bf16[64,256]{1,0:T(8,128)(2,1)}, bf16[64,256]{1,0:T(8,128)(2,1)S(1)}, u32[]{:S(2)}) copy-start(bf16[64,256]{1,0:T(8,128)(2,1)S(1)} %collective-permute-done.1.returned) | copy-start | bytes 98308
  26.6 2.8 %collective-permute-start.2 = (bf16[32,40,128]{2,1,0:T(8,128)(2,1)S(1)}, bf16[32,40,128]{2,1,0:T(8,128)(2,1)S(1)}, u32[]{:S(2)}, u32[]{:S(2)}) collective-permute-start(bf16[32,40,128]{2,1,0:T(8,128)(2,1)S(1)} %all-to-all-done.got_in), channel_id=1, source_target_pairs={{0,1},{1,0},{2,3},{3,2},{4,5},{5,4},{6,7},{7,6},{8,9},{9,8},{10,11... | collective-permute-start | bytes 983048 | tf_op jit(solution)/shard_map/ppermute | solution.py:610
  26.6 0.8 %copy-start.6 = (bf16[64,256]{1,0:T(8,128)(2,1)S(1)}, bf16[64,256]{1,0:T(8,128)(2,1)}, u32[]{:S(2)}) copy-start(bf16[64,256]{1,0:T(8,128)(2,1)} %copy-done.5) | copy-start | bytes 98308

commit v2 on v1

--- a/solution.py
+++ b/solution.py
@@ -350,6 +350,10 @@
         chains[:, c * 2 * rank : (c + 1) * 2 * rank] = jnp.concatenate(both, axis=0).T.astype(BF16)
 
 
+def halves_kernel(got, _, __, ___, out):
+    out[...] = got[:, : out.shape[1], :]
+
+
 def partner_rows(far_col, ref, side, count):
     pairs = far_col.shape[1]
     devices, _, wide = ref.shape
@@ -366,7 +370,7 @@
 
 
 def collect_kernel(
-    col_in, got_in, chains_in, root_in, own, returned, _, partner, arrived, down, near, far_col, got, chains, roots, sems
+    col_in, got_in, chains_in, root_in, own, returned, partner, arrived, down, near, far_col, got, chains, roots, sems
 ):
     devices, _, wide = got.shape
     count = arrived.shape[0]
@@ -413,15 +417,15 @@
 def finish_kernel(
     far_row,
     far_col,
-    sibling_in,
+    sibling,
     partner_in,
     arrived,
     down,
     near,
     bases,
+    coup_in,
+    out,
     coup,
-    out,
-    sibling,
     ahead,
     sems,
 ):
@@ -430,11 +434,14 @@
     count = rows // 2
     rank = wide // 2
     pairs = far_row.shape[1]
-    start_all([(sibling_in.at[:, pl.ds(0, sibling.shape[1])], sibling)], sems)[0].wait()
+    spans = [pl.ds(16 * g, 16) for g in range(rank // 16)]
+    copies = start_all([(coup_in.at[span], coup.at[span]) for span in spans], sems)
     side = 1 - lax.rem(lax.axis_index(AXES), 2)
     partner = (partner_in[...] + partner_rows(far_col, sibling, side, count)).T
 
     for r in range(rank):
+        if r % 16 == 0:
+            copies[r // 16].wait()
         block = coup[r]
         ahead[r : r + 1, :] = jnp.sum(block * partner[:rank], axis=0, keepdims=True)
         ahead[rank + r : rank + r + 1, :] = jnp.sum(block * partner[rank:], axis=0, keepdims=True)
@@ -535,7 +542,20 @@
     )(trans)
 
 
-def collect(far_col, got, chains, roots, own, returned, sign, count):
+def halves(got, chains, own, returned, count):
+    devices, _, wide = got.shape
+    return pl.pallas_call(
+        halves_kernel,
+        out_shape=jax.ShapeDtypeStruct((devices, count // 2, wide), BF16),
+        in_specs=[IN_VMEM] + [ANYWHERE] * 3,
+        out_specs=IN_VMEM,
+        compiler_params=SOME,
+        cost_estimate=cost(10**5, 10**5),
+        name="halves",
+    )(got, chains, own, returned)
+
+
+def collect(far_col, got, chains, roots, own, returned, count):
     wide = got.shape[2]
     fetched = (far_col, got, chains, roots)
     return pl.pallas_call(
@@ -546,30 +566,29 @@
             jax.ShapeDtypeStruct((16, chains.shape[1]), F32),
             jax.ShapeDtypeStruct(own.shape, F32),
         ),
-        in_specs=[IN_HBM] * 4 + [IN_VMEM] * 2 + [ANYWHERE],
+        in_specs=[IN_HBM] * 4 + [IN_VMEM] * 2,
         out_specs=(IN_VMEM,) * 4,
         scratch_shapes=[vmem(a) for a in fetched] + [pltpu.SemaphoreType.DMA((4,))],
         compiler_params=MOST,
         cost_estimate=cost(10**7, 3 * 10**6),
         name="collect",
-    )(far_col, got, chains, roots, own, returned, sign)
+    )(far_col, got, chains, roots, own, returned)
 
 
 def finish(far_row, far_col, sibling, partner, arrived, down, near, bases, coup):
     count = near.shape[0] // 2
-    devices, _, wide = sibling.shape
-    halves = jax.ShapeDtypeStruct((devices, count // 2, wide), BF16)
+    wide = sibling.shape[2]
     return pl.pallas_call(
         finish_kernel,
         out_shape=jax.ShapeDtypeStruct((count, 2, near.shape[1]), F32),
-        in_specs=[IN_VMEM] * 2 + [IN_HBM] + [IN_VMEM] * 6,
+        in_specs=[IN_VMEM] * 8 + [IN_HBM],
         out_specs=IN_VMEM,
         scratch_shapes=[
-            vmem(halves),
+            vmem(coup),
             pltpu.VMEM((wide, far_row.shape[1]), F32),
-            pltpu.SemaphoreType.DMA((1,)),
+            pltpu.SemaphoreType.DMA((coup.shape[0] // 16,)),
         ],
-        compiler_params=SOME,
+        compiler_params=pltpu.CompilerParams(vmem_limit_bytes=47 * 1024 * 1024),
         cost_estimate=cost(10**7, 5 * 10**6),
         name="finish",
     )(far_row, far_col, sibling, partner, arrived, down, near, bases, coup)
@@ -606,10 +625,10 @@
     own = near_main(*near, x, following, own, near_blocks, self_blocks)
     own, late_transfers = lax.optimization_barrier((own, transfers))
     chains = multiply_chains(late_transfers)
-    got, chains, sign = lax.optimization_barrier((got, chains, returned[:8]))
-    sibling = lax.ppermute(got, AXES, [(i, i ^ 1) for i in range(devices)])
+    mine = halves(got, chains, own, returned, count)
+    sibling = lax.ppermute(mine, AXES, [(i, i ^ 1) for i in range(devices)])
     partner, arrived, down, near_sum = collect(
-        far[1], got, chains, root_couplings[0], own, returned, sign, count
+        far[1], got, chains, root_couplings[0], own, returned, count
     )
     return finish(*far, sibling, partner, arrived, down, near_sum, flat_bases, coup)
 

time: 31.8 us -> 32.2 us (1.013)
  waiting for transfers between devices: 1.93 us -> 3 us
  local copies, waits for them, and re-layouts: 2.19 us -> 1.26 us
    unnamed x22 -> x18, local copies, waits for them, and re-layouts: 2.18 us -> 1.26 us
    ppermute x2, waiting for transfers between devices: 1.92 us -> 2.71 us  [from_behind(): lax.ppermute(x, AXES, [(i, (i + by) % devices) for i in range(devices)])]
  transfers between devices with their start and end apart: 4 -> 4, of which waited for: 1 -> 2; matrix products, arithmetic and copies ran while one was open for 0% -> 0% of each run, Pallas kernels for 50% -> 49%
where the time goes in v2:
time: 32.2 us; the launch traced here: 31.9 us
  Pallas kernels  18 us (56%)
  starting transfers between devices  9.54 us (30%)
  waiting for transfers between devices  3 us (9%)
  local copies, waits for them, and re-layouts  1.26 us (4%)
    ppermute x2, starting transfers between devices, from_behind(): lax.ppermute(x, AXES, [(i, (i + by) % devices) for i in range(devices)])  6.73 us
    pallas_call x1, Pallas kernels, near_main(): pl.pallas_call(near_main_kernel, out_shape=jax.ShapeDtypeStruct(own.shape...  4.81 us
    pallas_call x1, Pallas kernels, pack(): pl.pallas_call(pack_kernel, out_shape=jax.ShapeDtypeStruct((devices, coun...  4.76 us
    all_to_all x1, starting transfers between devices, shards(): got = lax.all_to_all(payload, AXES, 0, 0, tiled=True)  2.74 us
    ppermute x2, waiting for transfers between devices, from_behind(): lax.ppermute(x, AXES, [(i, (i + by) % devices) for i in range(devices)])  2.71 us
    pallas_call x1, Pallas kernels, near_back(): pl.pallas_call(near_back_kernel, out_shape=(jax.ShapeDtypeStruct((2 * cou...  2.7 us
    pallas_call x1, Pallas kernels, finish(): pl.pallas_call(finish_kernel, out_shape=jax.ShapeDtypeStruct((count, 2, n...  2.22 us
    pallas_call x1, Pallas kernels, collect(): pl.pallas_call(collect_kernel, out_shape=(jax.ShapeDtypeStruct((far_col.s...  2.02 us
  transfers between devices with their start and end apart: 4, of which 2 were waited for; matrix products, arithmetic and copies ran while one was open for 0% of the time, Pallas kernels for 49%

profile of v2, /device:TPU:0, one launch (start us, length us, event | category | flops | bytes accessed | tf_op | source)
XLA Modules:
  0.0 31.9 jit_solution(8329283663850072342)
XLA Ops:
  0.0 6.4 %collective-permute-start = (bf16[32,2,256]{2,1,0:T(2,128)(2,1)}, bf16[32,2,256]{2,1,0:T(2,128)(2,1)S(1)}, u32[]{:S(2)}, u32[]{:S(2)}) collective-permute-start(bf16[32,2,256]{2,1,0:T(2,128)(2,1)} %x_in.3), channel_id=1, source_target_pairs={{0,31},{1,0},{2,1},{3,2},{4,3},{5,4},{6,5},{7,6},{8,7},{9,8},{10,9... | collective-permute-start | bytes 98312 | tf_op jit(solution)/shard_map/ppermute | solution.py:17
  6.4 4.8 %pack.1 = bf16[32,40,128]{2,1,0:T(8,128)(2,1)} custom-call(s32[1,128]{1,0:T(1,128)} %bitcast.20, s32[1,128]{1,0:T(1,128)} %bitcast.13, bf16[32,2,256]{2,1,0:T(2,128)(2,1)} %x_in.3, bf16[2048,256]{1,0:T(8,128)(2,1)} %bitcast.11, f32[62,64,64]{2,1,0:T(8,128)} %trans, f32[64,64,128]{2,1,0:T(8,128)} %bitcast.9), custom_call_target="tpu_custom_call" | custom-call | flops 10000000 | bytes 6000000 | tf_op jit(solution)/shard_map/pack/pallas_call | solution.py:485
  11.2 0.0 collective-permute-done.after_in
  11.2 2.7 %all-to-all-start = ((bf16[32,40,128]{2,1,0:T(8,128)(2,1)}), bf16[32,40,128]{2,1,0:T(8,128)(2,1)S(1)}, u32[]{:S(2)}, u32[]{:S(2)}) async-start(bf16[32,40,128]{2,1,0:T(8,128)(2,1)} %pack.1), calls=%async_computation | async-start | bytes 655360 | tf_op jit(solution)/shard_map/all_to_all | solution.py:622
  14.0 0.0 copy-done.4
  14.0 0.0 copy-done.6
  14.0 2.7 %near_back.1 = (f32[64,256]{1,0:T(8,128)S(1)}, bf16[64,256]{1,0:T(8,128)(2,1)S(1)}) custom-call(s32[1,32]{1,0:T(1,128)S(1)} %bitcast.16, s32[1,32]{1,0:T(1,128)S(1)} %bitcast.18, bf16[32,2,256]{2,1,0:T(2,128)(2,1)S(1)} %copy-done.4, bf16[32,256,256]{2,1,0:T(8,128)(2,1)} %blocks_in.3), custom_call_target="tpu_custom_call" | custom-call | flops 10000000 | bytes 4000000 | tf_op jit(solution)/shard_map/near_back/pallas_call | solution.py:500
  16.7 0.3 collective-permute-start.1
  17.0 4.8 %near_main.1.__.own = f32[64,256]{1,0:T(8,128)S(1)} custom-call(s32[1,32]{1,0:T(1,128)S(1)} %bitcast.17, s32[1,32]{1,0:T(1,128)S(1)} %bitcast.19, bf16[32,2,256]{2,1,0:T(2,128)(2,1)S(1)} %copy-done.4, bf16[32,2,256]{2,1,0:T(2,128)(2,1)S(1)} %collective-permute-done.after_in, f32[64,256]{1,0:T(8,128)S(1)} %get-tuple-element.19.own_in, ...), custom_call_target="tpu_custom_call" | custom-call | flops 20000000 | bytes 8000000 | tf_op jit(solution)/shard_map/near_main/pallas_call | solution.py:518
  21.8 0.0 copy-done.1
  21.8 0.0 copy-start
  21.8 0.0 copy-start.8
  21.9 1.4 %chains.1._.chains_in = bf16[128,2048]{1,0:T(8,128)(2,1)S(1)} custom-call(f32[62,64,64]{2,1,0:T(8,128)S(1)} %copy-done.1), custom_call_target="tpu_custom_call" | custom-call | flops 10000000 | bytes 3000000 | tf_op jit(solution)/shard_map/chains/pallas_call | solution.py:534
  23.3 0.0 copy-start.2
  23.3 2.7 %collective-permute-done.1.___.returned = bf16[64,256]{1,0:T(8,128)(2,1)S(1)} collective-permute-done((bf16[64,256]{1,0:T(8,128)(2,1)S(1)}, bf16[64,256]{1,0:T(8,128)(2,1)S(1)}, u32[]{:S(2)}, u32[]{:S(2)}) %collective-permute-start.1) | collective-permute-done | bytes 32800 | tf_op jit(solution)/shard_map/ppermute | solution.py:17
  26.0 0.3 all-to-all-done.got.got_in
  26.3 0.1 collective-permute-start.2
  26.4 2.0 %collect.1 = (f32[128,128]{1,0:T(8,128)S(1)}, f32[32,128]{1,0:T(8,128)S(1)}, f32[16,2048]{1,0:T(8,128)S(1)}, f32[64,256]{1,0:T(8,128)S(1)}) custom-call(s32[1,128]{1,0:T(1,128)S(1)} %bitcast.14, bf16[32,40,128]{2,1,0:T(8,128)(2,1)S(1)} %all-to-all-done.got.got_in, bf16[128,2048]{1,0:T(8,128)(2,1)} %copy-done.2, f32[32,64,64]{2,1,0:T(8,128)} %bitcast.22, ...), custom_call_target="tpu_custom_call" | custom-call | flops 10000000 | bytes 3000000 | tf_op jit(solution)/shard_map/collect/pallas_call | solution.py:561
  28.4 0.0 collective-permute-done.2.sibling
  28.5 0.0 copy-done
  28.5 0.0 copy-done.8
  28.5 0.0 copy-start.3
  28.5 1.2 %copy-done.3 = bf16[32,256,64]{1,2,0:T(8,128)(2,1)S(1)} copy-done((bf16[32,256,64]{1,2,0:T(8,128)(2,1)S(1)}, bf16[32,256,64]{1,2,0:T(8,128)(2,1)}, u32[]{:S(2)}) %copy-start.3) | copy-done | bytes 1048600
  29.7 2.2 %finish.1 = f32[32,2,256]{2,1,0:T(2,128)} custom-call(s32[1,128]{1,0:T(1,128)S(1)} %bitcast.21, s32[1,128]{1,0:T(1,128)S(1)} %bitcast.15, bf16[32,16,128]{2,1,0:T(8,128)(2,1)S(1)} %collective-permute-done.2.sibling, f32[128,128]{1,0:T(8,128)S(1)} %get-tuple-element.23.partner_in, f32[32,128]{1,0:T(8,128)S(1)} %get-tuple-element.24.arrived, ...), custom_call_target="tpu_custom_call" | custom-call | flops 10000000 | bytes 5000000 | tf_op jit(solution)/shard_map/finish/pallas_call | solution.py:581
  (9 shorter events, 0.0 us)
Async XLA Ops:
  0.0 14.0 %copy-start.4 = (bf16[32,2,256]{2,1,0:T(2,128)(2,1)S(1)}, bf16[32,2,256]{2,1,0:T(2,128)(2,1)}, u32[]{:S(2)}) copy-start(bf16[32,2,256]{2,1,0:T(2,128)(2,1)} %x_in.3) | copy-start | bytes 98308
  0.0 14.0 %copy-start.6 = (s32[32]{0:T(128)S(1)}, s32[32]{0:T(128)}, u32[]{:S(2)}) copy-start(s32[32]{0:T(128)} %param.14) | copy-start | bytes 388
  0.0 14.0 %copy-start.7 = (s32[32]{0:T(128)S(1)}, s32[32]{0:T(128)}, u32[]{:S(2)}) copy-start(s32[32]{0:T(128)} %param.15) | copy-start | bytes 388
  0.0 11.2 %collective-permute-start = (bf16[32,2,256]{2,1,0:T(2,128)(2,1)}, bf16[32,2,256]{2,1,0:T(2,128)(2,1)S(1)}, u32[]{:S(2)}, u32[]{:S(2)}) collective-permute-start(bf16[32,2,256]{2,1,0:T(2,128)(2,1)} %x_in.3), channel_id=1, source_target_pairs={{0,31},{1,0},{2,1},{3,2},{4,3},{5,4},{6,5},{7,6},{8,7},{9,8},{10,9... | collective-permute-start | bytes 98312 | tf_op jit(solution)/shard_map/ppermute | solution.py:17
  11.2 15.1 %all-to-all-start = ((bf16[32,40,128]{2,1,0:T(8,128)(2,1)}), bf16[32,40,128]{2,1,0:T(8,128)(2,1)S(1)}, u32[]{:S(2)}, u32[]{:S(2)}) async-start(bf16[32,40,128]{2,1,0:T(8,128)(2,1)} %pack.1), calls=%async_computation | async-start | bytes 655360 | tf_op jit(solution)/shard_map/all_to_all | solution.py:622
  16.7 9.3 %collective-permute-start.1 = (bf16[64,256]{1,0:T(8,128)(2,1)S(1)}, bf16[64,256]{1,0:T(8,128)(2,1)S(1)}, u32[]{:S(2)}, u32[]{:S(2)}) collective-permute-start(bf16[64,256]{1,0:T(8,128)(2,1)S(1)} %get-tuple-element.22), channel_id=1, source_target_pairs={{0,1},{1,2},{2,3},{3,4},{4,5},{5,6},{6,7},{7,8},{8,9},{9,10},{10,1... | collective-permute-start | bytes 98312 | tf_op jit(solution)/shard_map/ppermute | solution.py:17
  17.0 4.8 %copy-start.1 = (f32[62,64,64]{2,1,0:T(8,128)S(1)}, f32[62,64,64]{2,1,0:T(8,128)}, u32[]{:S(2)}) copy-start(f32[62,64,64]{2,1,0:T(8,128)} %trans) | copy-start | bytes 3047428
  17.0 9.4 %copy-start.5 = (s32[128]{0:T(128)S(1)}, s32[128]{0:T(128)}, u32[]{:S(2)}) copy-start(s32[128]{0:T(128)} %param.19) | copy-start | bytes 1540
  21.8 6.6 %copy-start = (f32[128,64,64]{0,2,1:T(8,128)S(1)}, f32[128,64,64]{0,2,1:T(8,128)}, u32[]{:S(2)}) copy-start(f32[128,64,64]{0,2,1:T(8,128)} %param.20) | copy-start | bytes 6291460
  21.8 6.6 %copy-start.8 = (s32[128]{0:T(128)S(1)}, s32[128]{0:T(128)}, u32[]{:S(2)}) copy-start(s32[128]{0:T(128)} %param.18) | copy-start | bytes 1540
  23.3 3.1 %copy-start.2 = (bf16[128,2048]{1,0:T(8,128)(2,1)}, bf16[128,2048]{1,0:T(8,128)(2,1)S(1)}, u32[]{:S(2)}) copy-start(bf16[128,2048]{1,0:T(8,128)(2,1)S(1)} %chains.1._.chains_in) | copy-start | bytes 1572868
  26.3 2.1 %collective-permute-start.2 = (bf16[32,16,128]{2,1,0:T(8,128)(2,1)S(1)}, bf16[32,16,128]{2,1,0:T(8,128)(2,1)S(1)}, u32[]{:S(2)}, u32[]{:S(2)}) collective-permute-start(bf16[32,16,128]{2,1,0:T(8,128)(2,1)S(1)} %halves.1), channel_id=1, source_target_pairs={{0,1},{1,0},{2,3},{3,2},{4,5},{5,4},{6,7},{7,6},{8,9},{9,8},{10,11... | collective-permute-start | bytes 393224 | tf_op jit(solution)/shard_map/ppermute | solution.py:629
  28.5 1.2 %copy-start.3 = (bf16[32,256,64]{1,2,0:T(8,128)(2,1)S(1)}, bf16[32,256,64]{1,2,0:T(8,128)(2,1)}, u32[]{:S(2)}) copy-start(bf16[32,256,64]{1,2,0:T(8,128)(2,1)} %param.16) | copy-start | bytes 3145732

commit v3 on v2

--- a/solution.py
+++ b/solution.py
@@ -434,14 +434,14 @@
     count = rows // 2
     rank = wide // 2
     pairs = far_row.shape[1]
-    spans = [pl.ds(16 * g, 16) for g in range(rank // 16)]
+    spans = [pl.ds(8 * g, 8) for g in range(rank // 8)]
     copies = start_all([(coup_in.at[span], coup.at[span]) for span in spans], sems)
     side = 1 - lax.rem(lax.axis_index(AXES), 2)
     partner = (partner_in[...] + partner_rows(far_col, sibling, side, count)).T
 
     for r in range(rank):
-        if r % 16 == 0:
-            copies[r // 16].wait()
+        if r % 8 == 0:
+            copies[r // 8].wait()
         block = coup[r]
         ahead[r : r + 1, :] = jnp.sum(block * partner[:rank], axis=0, keepdims=True)
         ahead[rank + r : rank + r + 1, :] = jnp.sum(block * partner[rank:], axis=0, keepdims=True)
@@ -586,9 +586,9 @@
         scratch_shapes=[
             vmem(coup),
             pltpu.VMEM((wide, far_row.shape[1]), F32),
-            pltpu.SemaphoreType.DMA((coup.shape[0] // 16,)),
+            pltpu.SemaphoreType.DMA((coup.shape[0] // 8,)),
         ],
-        compiler_params=pltpu.CompilerParams(vmem_limit_bytes=47 * 1024 * 1024),
+        compiler_params=pltpu.CompilerParams(vmem_limit_bytes=51 * 1024 * 1024),
         cost_estimate=cost(10**7, 5 * 10**6),
         name="finish",
     )(far_row, far_col, sibling, partner, arrived, down, near, bases, coup)

time: 32.2 us -> 31.6 us (0.981)
  local copies, waits for them, and re-layouts: 1.26 us -> 0.04 us
  Pallas kernels: 18 us -> 18.6 us
    unnamed x18 -> x16, local copies, waits for them, and re-layouts: 1.26 us -> 0.04 us
    pallas_call x1, Pallas kernels: 2.22 us -> 2.9 us  [finish(): pl.pallas_call(finish_kernel, out_shape=jax.ShapeDtypeStruct((count, 2, n...]
  transfers between devices with their start and end apart: 4 -> 4, of which waited for: 2 -> 2; matrix products, arithmetic and copies ran while one was open for 0% -> 0% of each run, Pallas kernels for 49% -> 50%
where the time goes in v3:
time: 31.6 us; the launch traced here: 31.4 us
  Pallas kernels  18.6 us (59%)
  starting transfers between devices  9.53 us (30%)
  waiting for transfers between devices  3 us (9%)
    ppermute x2, starting transfers between devices, from_behind(): lax.ppermute(x, AXES, [(i, (i + by) % devices) for i in range(devices)])  6.73 us
    pallas_call x1, Pallas kernels, near_main(): pl.pallas_call(near_main_kernel, out_shape=jax.ShapeDtypeStruct(own.shape...  4.81 us
    pallas_call x1, Pallas kernels, pack(): pl.pallas_call(pack_kernel, out_shape=jax.ShapeDtypeStruct((devices, coun...  4.76 us
    pallas_call x1, Pallas kernels, finish(): pl.pallas_call(finish_kernel, out_shape=jax.ShapeDtypeStruct((count, 2, n...  2.9 us
    all_to_all x1, starting transfers between devices, shards(): got = lax.all_to_all(payload, AXES, 0, 0, tiled=True)  2.73 us
    ppermute x2, waiting for transfers between devices, from_behind(): lax.ppermute(x, AXES, [(i, (i + by) % devices) for i in range(devices)])  2.71 us
    pallas_call x1, Pallas kernels, near_back(): pl.pallas_call(near_back_kernel, out_shape=(jax.ShapeDtypeStruct((2 * cou...  2.7 us
    pallas_call x1, Pallas kernels, collect(): pl.pallas_call(collect_kernel, out_shape=(jax.ShapeDtypeStruct((far_col.s...  2.02 us
  transfers between devices with their start and end apart: 4, of which 2 were waited for; matrix products, arithmetic and copies ran while one was open for 0% of the time, Pallas kernels for 50%

profile of v3, /device:TPU:0, one launch (start us, length us, event | category | flops | bytes accessed | tf_op | source)
XLA Modules:
  0.0 31.4 jit_solution(2162467251583507440)
XLA Ops:
  0.0 6.4 %collective-permute-start = (bf16[32,2,256]{2,1,0:T(2,128)(2,1)}, bf16[32,2,256]{2,1,0:T(2,128)(2,1)S(1)}, u32[]{:S(2)}, u32[]{:S(2)}) collective-permute-start(bf16[32,2,256]{2,1,0:T(2,128)(2,1)} %x_in.3), channel_id=1, source_target_pairs={{0,31},{1,0},{2,1},{3,2},{4,3},{5,4},{6,5},{7,6},{8,7},{9,8},{10,9... | collective-permute-start | bytes 98312 | tf_op jit(solution)/shard_map/ppermute | solution.py:17
  6.4 4.8 %pack.1 = bf16[32,40,128]{2,1,0:T(8,128)(2,1)} custom-call(s32[1,128]{1,0:T(1,128)} %bitcast.18, s32[1,128]{1,0:T(1,128)} %bitcast.11, bf16[32,2,256]{2,1,0:T(2,128)(2,1)} %x_in.3, bf16[2048,256]{1,0:T(8,128)(2,1)} %bitcast.9, f32[62,64,64]{2,1,0:T(8,128)} %trans, f32[64,64,128]{2,1,0:T(8,128)} %bitcast.20), custom_call_target="tpu_custom_call" | custom-call | flops 10000000 | bytes 6000000 | tf_op jit(solution)/shard_map/pack/pallas_call | solution.py:485
  11.2 0.0 collective-permute-done.after_in
  11.2 2.7 %all-to-all-start = ((bf16[32,40,128]{2,1,0:T(8,128)(2,1)}), bf16[32,40,128]{2,1,0:T(8,128)(2,1)S(1)}, u32[]{:S(2)}, u32[]{:S(2)}) async-start(bf16[32,40,128]{2,1,0:T(8,128)(2,1)} %pack.1), calls=%async_computation | async-start | bytes 655360 | tf_op jit(solution)/shard_map/all_to_all | solution.py:622
  14.0 0.0 copy-done.3
  14.0 0.0 copy-done.5
  14.0 0.0 copy-done.6
  14.0 2.7 %near_back.1 = (f32[64,256]{1,0:T(8,128)S(1)}, bf16[64,256]{1,0:T(8,128)(2,1)S(1)}) custom-call(s32[1,32]{1,0:T(1,128)S(1)} %bitcast.14, s32[1,32]{1,0:T(1,128)S(1)} %bitcast.16, bf16[32,2,256]{2,1,0:T(2,128)(2,1)S(1)} %copy-done.3, bf16[32,256,256]{2,1,0:T(8,128)(2,1)} %blocks_in.3), custom_call_target="tpu_custom_call" | custom-call | flops 10000000 | bytes 4000000 | tf_op jit(solution)/shard_map/near_back/pallas_call | solution.py:500
  16.7 0.3 collective-permute-start.1
  17.0 4.8 %near_main.1.__.own = f32[64,256]{1,0:T(8,128)S(1)} custom-call(s32[1,32]{1,0:T(1,128)S(1)} %bitcast.15, s32[1,32]{1,0:T(1,128)S(1)} %bitcast.17, bf16[32,2,256]{2,1,0:T(2,128)(2,1)S(1)} %copy-done.3, bf16[32,2,256]{2,1,0:T(2,128)(2,1)S(1)} %collective-permute-done.after_in, f32[64,256]{1,0:T(8,128)S(1)} %get-tuple-element.19.own_in, ...), custom_call_target="tpu_custom_call" | custom-call | flops 20000000 | bytes 8000000 | tf_op jit(solution)/shard_map/near_main/pallas_call | solution.py:518
  21.8 0.0 copy-done
  21.8 0.0 copy-start.2
  21.8 0.0 copy-start.7
  21.9 1.4 %chains.1._.chains_in = bf16[128,2048]{1,0:T(8,128)(2,1)S(1)} custom-call(f32[62,64,64]{2,1,0:T(8,128)S(1)} %copy-done), custom_call_target="tpu_custom_call" | custom-call | flops 10000000 | bytes 3000000 | tf_op jit(solution)/shard_map/chains/pallas_call | solution.py:534
  23.3 0.0 copy-start.1
  23.3 2.7 %collective-permute-done.1.___.returned = bf16[64,256]{1,0:T(8,128)(2,1)S(1)} collective-permute-done((bf16[64,256]{1,0:T(8,128)(2,1)S(1)}, bf16[64,256]{1,0:T(8,128)(2,1)S(1)}, u32[]{:S(2)}, u32[]{:S(2)}) %collective-permute-start.1) | collective-permute-done | bytes 32800 | tf_op jit(solution)/shard_map/ppermute | solution.py:17
  26.0 0.3 all-to-all-done.got.got_in
  26.3 0.1 collective-permute-start.2
  26.4 0.0 copy-done.1
  26.4 2.0 %collect.1 = (f32[128,128]{1,0:T(8,128)S(1)}, f32[32,128]{1,0:T(8,128)S(1)}, f32[16,2048]{1,0:T(8,128)S(1)}, f32[64,256]{1,0:T(8,128)S(1)}) custom-call(s32[1,128]{1,0:T(1,128)S(1)} %bitcast.12, bf16[32,40,128]{2,1,0:T(8,128)(2,1)S(1)} %all-to-all-done.got.got_in, bf16[128,2048]{1,0:T(8,128)(2,1)} %copy-done.1, f32[32,64,64]{2,1,0:T(8,128)} %bitcast.22, ...), custom_call_target="tpu_custom_call" | custom-call | flops 10000000 | bytes 3000000 | tf_op jit(solution)/shard_map/collect/pallas_call | solution.py:561
  28.4 0.0 collective-permute-done.2.sibling
  28.5 0.0 copy-done.2
  28.5 0.0 copy-done.7
  28.5 2.9 %finish.1 = f32[32,2,256]{2,1,0:T(2,128)} custom-call(s32[1,128]{1,0:T(1,128)S(1)} %bitcast.19, s32[1,128]{1,0:T(1,128)S(1)} %bitcast.13, bf16[32,16,128]{2,1,0:T(8,128)(2,1)S(1)} %collective-permute-done.2.sibling, f32[128,128]{1,0:T(8,128)S(1)} %get-tuple-element.23.partner_in, f32[32,128]{1,0:T(8,128)S(1)} %get-tuple-element.24.arrived, ...), custom_call_target="tpu_custom_call" | custom-call | flops 10000000 | bytes 5000000 | tf_op jit(solution)/shard_map/finish/pallas_call | solution.py:581
  (7 shorter events, 0.0 us)
Async XLA Ops:
  0.0 14.0 %copy-start.3 = (bf16[32,2,256]{2,1,0:T(2,128)(2,1)S(1)}, bf16[32,2,256]{2,1,0:T(2,128)(2,1)}, u32[]{:S(2)}) copy-start(bf16[32,2,256]{2,1,0:T(2,128)(2,1)} %x_in.3) | copy-start | bytes 98308
  0.0 14.0 %copy-start.5 = (s32[32]{0:T(128)S(1)}, s32[32]{0:T(128)}, u32[]{:S(2)}) copy-start(s32[32]{0:T(128)} %param.14) | copy-start | bytes 388
  0.0 14.0 %copy-start.6 = (s32[32]{0:T(128)S(1)}, s32[32]{0:T(128)}, u32[]{:S(2)}) copy-start(s32[32]{0:T(128)} %param.15) | copy-start | bytes 388
  0.0 11.2 %collective-permute-start = (bf16[32,2,256]{2,1,0:T(2,128)(2,1)}, bf16[32,2,256]{2,1,0:T(2,128)(2,1)S(1)}, u32[]{:S(2)}, u32[]{:S(2)}) collective-permute-start(bf16[32,2,256]{2,1,0:T(2,128)(2,1)} %x_in.3), channel_id=1, source_target_pairs={{0,31},{1,0},{2,1},{3,2},{4,3},{5,4},{6,5},{7,6},{8,7},{9,8},{10,9... | collective-permute-start | bytes 98312 | tf_op jit(solution)/shard_map/ppermute | solution.py:17
  11.2 15.1 %all-to-all-start = ((bf16[32,40,128]{2,1,0:T(8,128)(2,1)}), bf16[32,40,128]{2,1,0:T(8,128)(2,1)S(1)}, u32[]{:S(2)}, u32[]{:S(2)}) async-start(bf16[32,40,128]{2,1,0:T(8,128)(2,1)} %pack.1), calls=%async_computation | async-start | bytes 655360 | tf_op jit(solution)/shard_map/all_to_all | solution.py:622
  16.7 9.3 %collective-permute-start.1 = (bf16[64,256]{1,0:T(8,128)(2,1)S(1)}, bf16[64,256]{1,0:T(8,128)(2,1)S(1)}, u32[]{:S(2)}, u32[]{:S(2)}) collective-permute-start(bf16[64,256]{1,0:T(8,128)(2,1)S(1)} %get-tuple-element.22), channel_id=1, source_target_pairs={{0,1},{1,2},{2,3},{3,4},{4,5},{5,6},{6,7},{7,8},{8,9},{9,10},{10,1... | collective-permute-start | bytes 98312 | tf_op jit(solution)/shard_map/ppermute | solution.py:17
  17.0 4.8 %copy-start = (f32[62,64,64]{2,1,0:T(8,128)S(1)}, f32[62,64,64]{2,1,0:T(8,128)}, u32[]{:S(2)}) copy-start(f32[62,64,64]{2,1,0:T(8,128)} %trans) | copy-start | bytes 3047428
  17.0 9.4 %copy-start.4 = (s32[128]{0:T(128)S(1)}, s32[128]{0:T(128)}, u32[]{:S(2)}) copy-start(s32[128]{0:T(128)} %param.19) | copy-start | bytes 1540
  21.8 6.6 %copy-start.2 = (bf16[32,256,64]{1,2,0:T(8,128)(2,1)S(1)}, bf16[32,256,64]{1,2,0:T(8,128)(2,1)}, u32[]{:S(2)}) copy-start(bf16[32,256,64]{1,2,0:T(8,128)(2,1)} %param.16) | copy-start | bytes 3145732
  21.8 6.6 %copy-start.7 = (s32[128]{0:T(128)S(1)}, s32[128]{0:T(128)}, u32[]{:S(2)}) copy-start(s32[128]{0:T(128)} %param.18) | copy-start | bytes 1540
  23.3 3.1 %copy-start.1 = (bf16[128,2048]{1,0:T(8,128)(2,1)}, bf16[128,2048]{1,0:T(8,128)(2,1)S(1)}, u32[]{:S(2)}) copy-start(bf16[128,2048]{1,0:T(8,128)(2,1)S(1)} %chains.1._.chains_in) | copy-start | bytes 1572868
  26.3 2.1 %collective-permute-start.2 = (bf16[32,16,128]{2,1,0:T(8,128)(2,1)S(1)}, bf16[32,16,128]{2,1,0:T(8,128)(2,1)S(1)}, u32[]{:S(2)}, u32[]{:S(2)}) collective-permute-start(bf16[32,16,128]{2,1,0:T(8,128)(2,1)S(1)} %halves.1), channel_id=1, source_target_pairs={{0,1},{1,0},{2,3},{3,2},{4,5},{5,4},{6,7},{7,6},{8,9},{9,8},{10,11... | collective-permute-start | bytes 393224 | tf_op jit(solution)/shard_map/ppermute | solution.py:629
